TPU v7x, 256 devices: a whole 4x4x8 slice. The times are simulated.
256 devices in a mesh: dp: 2 (over core), seq: 4 (over x), head: 32 (over z, y).
Axes of the slice: x: 4, y: 4, z: 8, core: 2. Of those that a mesh axis runs over, the one named last changes fastest.
Arguments:
- tokens_in: bfloat16 [32768, 3072], P(('dp', 'head'), 'seq'), parts along dimension 0, may hold values from -6 to 6
- qkv_weight: bfloat16 [3072, 3, 1536], P('head', None, 'seq'), may hold values from -0.109375 to 0.109375
- norm_gains: float32 [2, 128], replicated, may hold values from 0.1 to 1.9
- out_weight: bfloat16 [3072, 1536], P('seq', 'head'), may hold values from -0.15625 to 0.15625
- neighbours: int32 [256, 10], P(('dp', 'head')), parts along dimension 0, may hold values from -1 to 127, as said below
Outputs:
- attended: bfloat16 [32768, 3072], P(('dp', 'head'), 'seq'), parts along dimension 0
There are 2 independent parts, one for each index of `dp`. A program takes and returns all parts, laid end to end along the dimension named above; an argument that names none is the same for every part. Nothing has to cross between parts.
Inputs may be any that keep to these rules, and one draw needn't show every extreme that they name: `neighbours`: tiles are numbered in raster order over a clip of 32 x 2 x 2 tiles. Slot 0 of row t is t itself; the other slots name distinct tiles other than t that lie within one tile of t along each of the three dimensions, or -1, in no particular order.
All inputs are finite; a program needn't handle non-finite values.
Results may differ from a plain program's by a relative error of at most 0.008.
Values may be sent and summed in bfloat16 or wider, within the bound.
No kernel may reach another device: no remote copies, remote signals or barrier semaphores. Data moves between devices by JAX's collectives and lax.ppermute only.
A program may use at most 64 MiB of HBM per device.

v0:
```python
import jax
import jax.numpy as jnp
from jax import lax
from jax.sharding import PartitionSpec as P

HD = 128
TILE = 128
HT = 2
WT = 2
WIN = 10


def extended_2(x, sides, width):
    for axis, dim in sides:
        count, length = (lax.axis_size(axis), x.shape[dim])
        up = [(i, (i + 1) % count) for i in range(count - 1)]
        down = [(j, i) for i, j in up]
        last = lax.slice_in_dim(x, length - width, length, axis=dim)
        initial = lax.slice_in_dim(x, 0, width, axis=dim)
        before = lax.ppermute(last, axis, up)
        after = lax.ppermute(initial, axis, down)
        x = jnp.concatenate([before, x, after], axis=dim)
    return x


def rms_normed(values, gain):
    mean_sq = jnp.mean(values * values, axis=-1, keepdims=True)
    return values * lax.rsqrt(mean_sq + 1e-06) * gain


def per_device(tokens_in, qkv_weight, norm_gains, out_weight, neighbours):
    whole = lax.all_gather(tokens_in, "seq", axis=1, tiled=True)
    rows = whole.shape[0]
    width = qkv_weight.shape[2]
    heads_here = width // HD
    tiles_here = rows // TILE
    frame_tiles = HT * WT
    scale = HD ** (-0.5)
    piece = lax.all_gather(qkv_weight, "head", axis=0, tiled=True)
    flat = piece.reshape(piece.shape[0], 3 * width)
    projected = jnp.dot(whole, flat, preferred_element_type=jnp.float32)
    projected = projected.reshape(rows, 3, heads_here, HD)
    query_normed = rms_normed(projected[:, 0], norm_gains[0]).astype(jnp.bfloat16)
    key_normed = rms_normed(projected[:, 1], norm_gains[1]).astype(jnp.bfloat16)
    value_rounded = projected[:, 2].astype(jnp.bfloat16)
    packed = jnp.concatenate(
        [key_normed.reshape(rows, width), value_rounded.reshape(rows, width)], axis=1
    )
    extended = extended_2(packed, (("head", 0),), frame_tiles * TILE)
    query_tiles = query_normed.reshape(tiles_here, TILE, heads_here, HD)
    extended_tiles = extended.shape[0] // TILE
    first_tile = lax.axis_index("head") * tiles_here - frame_tiles
    local_index = jnp.where(neighbours >= 0, neighbours - first_tile, 0)
    local_index = jnp.clip(local_index, 0, extended_tiles - 1)
    gathered_pack = extended.reshape(extended_tiles, TILE, 2 * width)[local_index]
    gathered_pack = gathered_pack.reshape(tiles_here, WIN * TILE, 2, heads_here, HD)
    key_pick = gathered_pack[:, :, 0]
    value_pick = gathered_pack[:, :, 1]
    score = (
        jnp.einsum("tqhd,tkhd->thqk", query_tiles, key_pick, preferred_element_type=jnp.float32)
        * scale
    )
    keep = jnp.repeat(neighbours >= 0, TILE, axis=1)
    weight_exp = jnp.where(keep[:, None, None, :], jnp.exp(score), 0.0).astype(jnp.bfloat16)
    numer = jnp.einsum(
        "thqk,tkhd->tqhd", weight_exp, value_pick, preferred_element_type=jnp.float32
    )
    denom = jnp.transpose(jnp.sum(weight_exp.astype(jnp.float32), axis=-1), (0, 2, 1))
    head_out = (numer / denom[..., None]).astype(jnp.bfloat16).reshape(rows, width)
    head_all = lax.all_gather(head_out, "seq", axis=1, tiled=True)
    attended = jnp.einsum(
        "rc,ec->re",
        head_all,
        lax.all_gather(out_weight, "head", axis=1, tiled=True),
        preferred_element_type=jnp.float32,
    )
    return attended.astype(jnp.bfloat16)


def solution(mesh):
    placed = (
        P(("dp", "head"), "seq"),
        P("head", None, "seq"),
        P(),
        P("seq", "head"),
        P(("dp", "head"), None),
    )
    return jax.shard_map(
        per_device, mesh=mesh, in_specs=placed, out_specs=P(("dp", "head"), "seq"), check_vma=False
    )
```

profile of v0, /device:TPU:1, one launch (start us, length us, event | category | flops | bytes accessed | tf_op | source)
XLA Modules:
  0.0 284.8 jit_solution(8307151149664268340)
XLA Ops:
  6.5 0.7 all-gather.7.cloned.1.call-update
  8.8 0.8 slice_bitcast_fusion
  9.6 95.9 %all-gather.7.cloned.1.call-done = bf16[3072,3,384]{2,0,1:T(8,128)(2,1)} async-done(((bf16[96,3,384]{2,0,1:T(8,128)(2,1)}), bf16[3072,3,384]{2,0,1:T(8,128)(2,1)}) %all-gather.7.cloned.1.call-update) | async-done | bytes 7077904 | tf_op jit(solution)/shard_map/all_gather | solution.py:39
  105.4 10.1 %copy.24 = bf16[3072,3,384]{0,2,1:T(8,128)(2,1)} copy(bf16[3072,3,384]{2,0,1:T(8,128)(2,1)} %all-gather.7.cloned.1.call-done) | data formatting | bytes 14155776 | tf_op jit(solution)/shard_map/all_gather | solution.py:39
  115.5 31.3 %all-gather.5.cloned.1.call-done = bf16[512,3072]{1,0:T(8,128)(2,1)} async-done(((bf16[512,768]{1,0:T(8,128)(2,1)}), bf16[512,3072]{1,0:T(8,128)(2,1)}) %all-gather.5.cloned.1.call-update) | async-done | bytes 3145744 | tf_op jit(solution)/shard_map/all_gather | solution.py:32
  146.8 7.0 %fusion.2 = f32[512,3,3,128]{0,3,2,1:T(8,128)S(1)} fusion(bf16[3,3,128,3072]{3,2,1,0:T(8,128)(2,1)} %bitcast.72, bf16[512,3072]{1,0:T(8,128)(2,1)} %all-gather.5.cloned.1.call-done), kind=kOutput, calls=%fused_computation.6 | convolution fusion | flops 3623878656 | bytes 12582912 | tf_op jit(solution)/shard_map/dot_general | solution.py:41
  154.4 0.9 pad_maximum_fusion.1
  155.4 3.2 %collective-permute-start = (bf16[512,768]{0,1:T(8,128)(2,1)}, bf16[512,768]{0,1:T(8,128)(2,1)S(1)}, u32[]{:S(2)}, u32[]{:S(2)}) collective-permute-start(bf16[512,768]{0,1:T(8,128)(2,1)} %pad_maximum_fusion.1), channel_id=1, source_target_pairs={{0,1},{1,2},{2,3},{3,4},{4,5},{5,6},{6,7},{7,8},{8,9},{9,10},{10,1... | collective-permute-start | bytes 2359304 | tf_op jit(solution)/shard_map/ppermute | solution.py:20
  158.5 1.5 collective-permute-start.1
  160.5 1.2 copy.29
  161.7 14.1 %collective-permute-done = bf16[512,768]{0,1:T(8,128)(2,1)S(1)} collective-permute-done((bf16[512,768]{0,1:T(8,128)(2,1)}, bf16[512,768]{0,1:T(8,128)(2,1)S(1)}, u32[]{:S(2)}, u32[]{:S(2)}) %collective-permute-start) | collective-permute-done | bytes 786464 | tf_op jit(solution)/shard_map/ppermute | solution.py:20
  175.9 4.1 %collective-permute-done.1 = bf16[512,768]{0,1:T(8,128)(2,1)} collective-permute-done((bf16[512,768]{0,1:T(8,128)(2,1)}, bf16[512,768]{0,1:T(8,128)(2,1)}, u32[]{:S(2)}, u32[]{:S(2)}) %collective-permute-start.1) | collective-permute-done | bytes 786464 | tf_op jit(solution)/shard_map/ppermute | solution.py:21
  179.9 2.7 pad_maximum_fusion
  182.6 2.8 copy.25
  185.5 5.8 %gather_fusion = bf16[40,128,768]{2,1,0:T(8,128)(2,1)} fusion(bf16[12,128,768]{2,1,0:T(8,128)(2,1)S(1)} %bitcast.71, s32[1024]{0:T(1024)S(1)} %pad_clamp_fusion), kind=kCustom, calls=%fused_computation | custom fusion | bytes 15728800 | tf_op jit(solution)/shard_map/gather | solution.py:55
  191.3 10.9 %copy.26 = bf16[40,128,768]{1,0,2:T(8,128)(2,1)} copy(bf16[40,128,768]{2,1,0:T(8,128)(2,1)} %gather_fusion) | data formatting | bytes 15728640 | tf_op jit(solution)/shard_map/gather | solution.py:55
  202.2 14.4 %reshape.55 = bf16[4,1280,2,3,128]{1,0,4,3,2:T(4,128)(2,1)} reshape(bf16[40,128,768]{1,0,2:T(8,128)(2,1)} %copy.26) | data formatting | bytes 15728640 | tf_op jit(solution)/shard_map/reshape | solution.py:56
  216.6 7.9 %fusion.11 = (bf16[4,1280,1,3,128]{1,0,4,3,2:T(4,128)(2,1)}, bf16[4,1280,1,3,128]{1,0,4,3,2:T(4,128)(2,1)}) fusion(bf16[4,1280,2,3,128]{1,0,4,3,2:T(4,128)(2,1)} %reshape.55), kind=kLoop, calls=%fused_computation.34 | loop fusion | bytes 15728640 | tf_op jit(solution)/shard_map/slice | solution.py:58
  224.5 8.6 %copy.34 = bf16[4,1280,1,3,128]{4,1,3,0,2:T(8,128)(2,1)} copy(bf16[4,1280,1,3,128]{1,0,4,3,2:T(4,128)(2,1)} %get-tuple-element.8) | data formatting | bytes 7864320
  233.1 4.5 %convert_reduce_fusion = (f32[4,3,128]{2,1,0:T(4,128)S(1)}, bf16[4,3,128,1280]{3,2,1,0:T(8,128)(2,1)S(1)}) fusion(bf16[4,1280,1,3,128]{4,1,3,0,2:T(8,128)(2,1)} %copy.34, f32[4,128,3,128]{3,1,2,0:T(8,128)S(1)} %copy-done.1, f32[128]{0:T(128)S(1)} %get-tuple-element.11, f32[4,128,3]{1,2,0:T(4,128)S(1)} %rsqrt_bitcast_fusion, pred[4,1280]{1,0:T(4,128)(4,1)S(1)} %bitcast.77), kind=kOutput, calls=%fused_computation.1 | convolution fusion | flops 513735168 | bytes 8668672 | tf_op jit(solution)/shard_map/tqhd,tkhd->thqk/dot_general | solution.py:60
  237.6 1.2 fusion.6
  239.1 0.8 copy.47
  240.0 33.8 %all-gather.9.cloned.1.call-done = bf16[512,1536]{0,1:T(8,128)(2,1)} async-done(((bf16[512,384]{0,1:T(8,128)(2,1)}), bf16[512,1536]{0,1:T(8,128)(2,1)}) %all-gather.9.cloned.1.call-update) | async-done | bytes 1572880 | tf_op jit(solution)/shard_map/all_gather | solution.py:70
  273.8 4.5 %convolution_convert_fusion = bf16[512,768]{1,0:T(8,128)(2,1)} fusion(bf16[512,1536]{0,1:T(8,128)(2,1)} %all-gather.9.cloned.1.call-done, bf16[768,1536]{0,1:T(8,128)(2,1)} %all-gather.11.cloned.1.call-done), kind=kOutput, calls=%fused_computation.9 | convolution fusion | flops 1208352768 | bytes 4718592 | tf_op jit(solution)/shard_map/rc,ec->re/dot_general | solution.py:71
  (28 shorter events, 2.8 us)
Async XLA Ops:
  6.5 98.9 %all-gather.7.cloned.1.call-start = ((), (), s32[]{:S(2)}) async-start(), calls=%async_computation.1 | async-start | bytes 7299072 | tf_op jit(solution)/shard_map/all_gather | solution.py:39
  7.3 139.6 %all-gather.5.cloned.1.call-start = ((), (), s32[]{:S(2)}) async-start(), calls=%async_computation | async-start | bytes 3932160 | tf_op jit(solution)/shard_map/all_gather | solution.py:32
  8.0 232.0 %all-gather.11.cloned.1.call-start = ((), (), s32[]{:S(2)}) async-start(), calls=%async_computation.3 | async-start | bytes 2433024 | tf_op jit(solution)/shard_map/all_gather | solution.py:74
  8.7 265.1 %all-gather.9.cloned.1.call-start = ((), (), s32[]{:S(2)}) async-start(), calls=%async_computation.2 | async-start | bytes 1966080 | tf_op jit(solution)/shard_map/all_gather | solution.py:70
  153.9 6.1 %copy-start.2 = (s32[4,10]{1,0:T(4,128)S(1)}, s32[4,10]{1,0:T(4,128)}, u32[]{:S(2)}) copy-start(s32[4,10]{1,0:T(4,128)} %param.9) | copy-start | bytes 484
  155.4 20.5 %collective-permute-start = (bf16[512,768]{0,1:T(8,128)(2,1)}, bf16[512,768]{0,1:T(8,128)(2,1)S(1)}, u32[]{:S(2)}, u32[]{:S(2)}) collective-permute-start(bf16[512,768]{0,1:T(8,128)(2,1)} %pad_maximum_fusion.1), channel_id=1, source_target_pairs={{0,1},{1,2},{2,3},{3,4},{4,5},{5,6},{6,7},{7,8},{8,9},{9,10},{10,1... | collective-permute-start | bytes 2359304 | tf_op jit(solution)/shard_map/ppermute | solution.py:20
  158.5 21.4 %collective-permute-start.1 = (bf16[512,768]{0,1:T(8,128)(2,1)}, bf16[512,768]{0,1:T(8,128)(2,1)}, u32[]{:S(2)}, u32[]{:S(2)}) collective-permute-start(bf16[512,768]{0,1:T(8,128)(2,1)} %pad_maximum_fusion.1), channel_id=1, source_target_pairs={{1,0},{2,1},{3,2},{4,3},{5,4},{6,5},{7,6},{8,7},{9,8},{10,9},{11,1... | collective-permute-start | bytes 2359304 | tf_op jit(solution)/shard_map/ppermute | solution.py:21
  224.5 8.6 %copy-start.1 = (f32[4,128,3,128]{3,1,2,0:T(8,128)S(1)}, f32[4,128,3,128]{3,1,2,0:T(8,128)}, u32[]{:S(2)}) copy-start(f32[4,128,3,128]{3,1,2,0:T(8,128)} %copy.29) | copy-start | bytes 2359300
  233.1 4.5 %copy-start = (bf16[4,1280,1,3,128]{1,0,4,3,2:T(4,128)(2,1)S(1)}, bf16[4,1280,1,3,128]{1,0,4,3,2:T(4,128)(2,1)}, u32[]{:S(2)}) copy-start(bf16[4,1280,1,3,128]{1,0,4,3,2:T(4,128)(2,1)} %get-tuple-element.7) | copy-start | bytes 11796484
Sparse Core Ops, SparseCore 0:
  9.9 95.4 all-gather.6
  107.2 39.5 all-gather.4
  149.4 75.1 all-gather.10
  240.1 33.6 all-gather.8
where the time goes:
time: 286 us; the launch traced here: 285 us
  waiting for transfers between devices  181 us (63%)
  local copies, waits for them, and re-layouts  64.2 us (22%)
  matrix products  17.2 us (6%)
  between operations  13.3 us (5%)
  starting transfers between devices  4.74 us (2%)
  other arithmetic  4.11 us (1%)
    all_gather x1, waiting for transfers between devices, per_device(): piece = lax.all_gather(qkv_weight, 'head', axis=0, tiled=True)  95.9 us
    all_gather x1, waiting for transfers between devices, per_device(): head_all = lax.all_gather(head_out, 'seq', axis=1, tiled=True)  33.8 us
    all_gather x1, waiting for transfers between devices, per_device(): whole = lax.all_gather(tokens_in, 'seq', axis=1, tiled=True)  31.3 us
    gather x2, local copies, waits for them, and re-layouts, per_device(): extended.reshape(extended_tiles, TILE, 2 * width)[local_index]  16.7 us
    reshape x1, local copies, waits for them, and re-layouts, per_device(): gathered_pack.reshape(tiles_here, WIN * TILE, 2, heads_here, HD)  14.4 us
    ppermute x1, waiting for transfers between devices, extended_2(): before = lax.ppermute(last, axis, up)  14.1 us
    all_gather x1, local copies, waits for them, and re-layouts, per_device(): piece = lax.all_gather(qkv_weight, 'head', axis=0, tiled=True)  10.1 us
    unnamed x10, local copies, waits for them, and re-layouts  9.52 us
  transfers between devices with their start and end apart: 6, of which 5 were waited for; matrix products, arithmetic and copies ran while one was open for 28% of the time, Pallas kernels for 0%

commit v1 on v0

v1 whole, which is shorter than its diff:
```python
import functools
import math

import jax
import jax.numpy as jnp
from jax import lax
from jax.experimental import pallas as pl
from jax.experimental.pallas import tpu as pltpu
from jax.sharding import PartitionSpec as P

HD = 128
TILE = 128
FRAME = 4
NY, NZ = 4, 8
BF = jnp.bfloat16
ANY = pl.BlockSpec(memory_space=pl.ANY)
VMEM = pl.BlockSpec(memory_space=pltpu.VMEM)
SMEM = pl.BlockSpec(memory_space=pltpu.SMEM)
LIMIT = 48 * 1024 * 1024

Y_FIRST_SUB = (0, -1, 1, 2)
Z_FIRST_SUB = (0, -2, 2, 4)
Y_FIRST_BUF = (0, -1, 1, -2, 2, -3, 3, -4)
Z_FIRST_BUF = ((0, 0), (1, 0), (0, 1), (1, -1), (0, 2), (1, -2), (0, 3), (1, -3))


def moved(x, core0, core1):
    pairs = []
    for core, (dz, dy) in enumerate((core0, core1)):
        for z in range(NZ):
            for y in range(NY):
                target = ((z + dz) % NZ) * NY + (y + dy) % NY
                pairs.append((core * NZ * NY + z * NY + y, core * NZ * NY + target))
    return lax.ppermute(x, ("dp", "head"), pairs)


def along(x, axis, step):
    n = lax.axis_size(axis)
    return lax.ppermute(x, axis, [(i, (i + step) % n) for i in range(n)])


def swapped(x):
    return lax.ppermute(x, "dp", [(0, 1), (1, 0)])


def ring_x(x):
    half = x.shape[0] // 2
    below = along(x, "seq", 1)
    above = along(x, "seq", -1)
    far_top = along(below[:half], "seq", 1)
    far_bottom = along(above[half:], "seq", -1)
    return below, above, far_top, far_bottom


def weight_buffers(mine):
    a = moved(mine, (0, 1), (2, 0))
    b = moved(mine, (0, -1), (-2, 0))
    c = moved(mine, (0, 2), (4, 0))
    start = jnp.concatenate([mine, a, b, c], axis=1)
    p1 = moved(start, (1, 0), (-1, 0))
    p2 = moved(start, (-1, 0), (0, -1))
    p3 = moved(p1, (1, 0), (0, 1))
    p4 = moved(p2, (-1, 0), (0, -1))
    p5 = moved(p3, (1, 0), (0, 1))
    p6 = moved(p4, (-1, 0), (0, -1))
    p7 = moved(p5, (1, 0), (0, 1))
    return [start, p1, p2, p3, p4, p5, p6, p7]


def row_table(z, y, core, rows):
    table = []
    for k in range(8):
        for i in range(4):
            z0, y0 = (z + Y_FIRST_BUF[k]) % NZ, (y + Y_FIRST_SUB[i]) % NY
            z1 = (z + Z_FIRST_BUF[k][0] + Z_FIRST_SUB[i]) % NZ
            y1 = (y + Z_FIRST_BUF[k][1]) % NY
            block = jnp.where(core == 0, z0 * NY + y0, z1 * NY + y1)
            table.append((block * 2 + core) * rows)
    return table


def normed(values, gain):
    mean_sq = jnp.mean(values * values, axis=-1, keepdims=True)
    return (values * lax.rsqrt(mean_sq + 1e-06) * gain).astype(BF)


def project_kernel(rows, place, token_place, *refs):
    gains = refs[0]
    tokens = refs[1:6]
    weights = refs[6:22]
    q_ref, kv_ref = refs[22:24]
    x, w, x_sem, w_sem = refs[24:]
    feats = tokens[0].shape[1]
    half = tokens[3].shape[0]
    copies = []
    starts = (0, 0, 0, 0, half)
    for i, ref in enumerate(tokens):
        n = ref.shape[0]
        at = pl.multiple_of(token_place[i], 128)
        copies.append(
            pltpu.make_async_copy(ref, x.at[pl.ds(starts[i], n), pl.ds(at, feats)], x_sem.at[i])
        )
    for k, ref in enumerate(weights):
        for i in range(4):
            at = pl.multiple_of(place[k * 4 + i], 16)
            copies.append(
                pltpu.make_async_copy(
                    ref.at[:, pl.ds(i * rows, rows), :], w.at[:, pl.ds(at, rows), :], w_sem.at[k, i]
                )
            )
    for c in copies:
        c.start()
    for c in copies:
        c.wait()
    heads = q_ref.shape[1] // HD
    for j in range(3):
        out = jnp.dot(x[...], w[j], preferred_element_type=jnp.float32)
        for h in range(heads):
            part = out[:, h * HD : (h + 1) * HD]
            if j == 0:
                q_ref[:, h * HD : (h + 1) * HD] = normed(part, gains[0:1, :])
            elif j == 1:
                kv_ref[:, h * HD : (h + 1) * HD] = normed(part, gains[1:2, :])
            else:
                at = (heads + h) * HD
                kv_ref[:, at : at + HD] = part.astype(BF)


def project(place, token_place, gains, tokens, weights):
    rows_here, feats = tokens[0].shape
    width = weights[0].shape[2]
    rows = weights[0].shape[1] // 4
    depth = 4 * feats
    return pl.pallas_call(
        functools.partial(project_kernel, rows),
        out_shape=(
            jax.ShapeDtypeStruct((rows_here, width), BF),
            jax.ShapeDtypeStruct((rows_here, 2 * width), BF),
        ),
        in_specs=[SMEM, SMEM, VMEM] + [ANY] * (5 + 16),
        out_specs=(VMEM, VMEM),
        scratch_shapes=[
            pltpu.VMEM((rows_here, depth), BF),
            pltpu.VMEM((3, depth, width), BF),
            pltpu.SemaphoreType.DMA((5,)),
            pltpu.SemaphoreType.DMA((16, 4)),
        ],
        compiler_params=pltpu.CompilerParams(vmem_limit_bytes=LIMIT),
        cost_estimate=pl.CostEstimate(
            flops=2 * rows_here * depth * 3 * width, bytes_accessed=12 * 2**20, transcendentals=0
        ),
        name="project",
    )(place, token_place, gains, *tokens, *weights)


def attend_frame(q, kv, keep, acc, heads, scale):
    rows, keys = q.shape[0], kv.shape[0]
    ones = jnp.ones((keys, HD), BF)
    out = []
    for h in range(heads):
        score = lax.dot_general(
            q[:, h * HD : (h + 1) * HD],
            kv[:, h * HD : (h + 1) * HD],
            (((1,), (1,)), ((), ())),
            preferred_element_type=jnp.float32,
        )
        weight = jnp.exp2(score * scale).reshape(rows // TILE, TILE, keys)
        weight = jnp.where(keep[:, None, :] > 0, weight, 0.0).reshape(rows, keys).astype(BF)
        at = (heads + h) * HD
        value = jnp.concatenate([kv[:, at : at + HD], ones], axis=1)
        part = jnp.dot(weight, value, preferred_element_type=jnp.float32)
        out.append(part if acc is None else acc[h] + part)
    return out


def own_kernel(heads, scale, q_ref, kv_ref, keep_ref, acc_ref):
    parts = attend_frame(q_ref, kv_ref, keep_ref[...], None, heads, scale)
    for h in range(heads):
        acc_ref[h] = parts[h]


def rest_kernel(heads, scale, q_ref, before_ref, after_ref, keep_ref, acc_ref, out_ref):
    keys = before_ref.shape[0]
    acc = [acc_ref[h] for h in range(heads)]
    acc = attend_frame(q_ref, before_ref, keep_ref[:, :keys], acc, heads, scale)
    acc = attend_frame(q_ref, after_ref, keep_ref[:, keys:], acc, heads, scale)
    for h in range(heads):
        out_ref[:, h * HD : (h + 1) * HD] = (acc[h][:, :HD] / acc[h][:, HD:]).astype(BF)


def local_call(kernel, out_shape, n_in, flops, nbytes, name):
    return pl.pallas_call(
        kernel,
        out_shape=out_shape,
        in_specs=[VMEM] * n_in,
        out_specs=VMEM,
        compiler_params=pltpu.CompilerParams(vmem_limit_bytes=LIMIT),
        cost_estimate=pl.CostEstimate(flops=flops, bytes_accessed=nbytes, transcendentals=0),
        name=name,
    )


def output_kernel(place, own, below, above, far_top, far_bottom, w_ref, out_ref, x, sem):
    feats = own.shape[1]
    half = far_top.shape[0]
    copies = []
    for i, (ref, start) in enumerate(
        ((own, 0), (below, 0), (above, 0), (far_top, 0), (far_bottom, half))
    ):
        at = pl.multiple_of(place[i], 128)
        copies.append(
            pltpu.make_async_copy(
                ref, x.at[pl.ds(start, ref.shape[0]), pl.ds(at, feats)], sem.at[i]
            )
        )
    for c in copies:
        c.start()
    for c in copies:
        c.wait()
    out_ref[...] = jnp.dot(x[...], w_ref[...], preferred_element_type=jnp.float32).astype(BF)


def output_projection(place, pieces, weight):
    rows, feats = pieces[0].shape
    depth, width = weight.shape
    return pl.pallas_call(
        output_kernel,
        out_shape=jax.ShapeDtypeStruct((rows, width), BF),
        in_specs=[SMEM] + [ANY] * 5 + [VMEM],
        out_specs=VMEM,
        scratch_shapes=[pltpu.VMEM((rows, depth), BF), pltpu.SemaphoreType.DMA((5,))],
        compiler_params=pltpu.CompilerParams(vmem_limit_bytes=LIMIT),
        cost_estimate=pl.CostEstimate(
            flops=2 * rows * depth * width, bytes_accessed=5 * 2**20, transcendentals=0
        ),
        name="output",
    )(place, *pieces, weight)


def per_device(tokens_in, qkv_weight, norm_gains, out_weight, neighbours):
    rows = tokens_in.shape[0]
    width = qkv_weight.shape[2]
    heads = width // HD
    tiles = rows // TILE
    core, seq, head = lax.axis_index("dp"), lax.axis_index("seq"), lax.axis_index("head")
    z, y = head // NY, head % NY
    half = qkv_weight.shape[0] // 2
    feats = tokens_in.shape[1]

    seq_of = jnp.stack([(seq + d) % 4 for d in (0, -1, 1, 2, 2)]).astype(jnp.int32)
    place = jnp.stack(
        row_table(z, y, core, half) + row_table(z, y, 1 - core, half)
    ).astype(jnp.int32)
    listed = neighbours[:, :, None] == (head * FRAME - FRAME + jnp.arange(3 * FRAME))[None, None, :]
    listed = listed & (neighbours >= 0)[:, :, None]
    keep = jnp.repeat(jnp.any(listed, axis=1), TILE, axis=1).astype(jnp.float32)
    keys = FRAME * TILE

    out_all = lax.all_gather(jnp.transpose(out_weight), "head", axis=0, tiled=True)
    mine = lax.dynamic_slice_in_dim(jnp.transpose(qkv_weight, (1, 0, 2)), core * half, half, axis=1)
    buffers = weight_buffers(mine)
    tokens = (tokens_in,) + ring_x(tokens_in)
    weights = buffers + [swapped(b) for b in buffers]
    query, kv = project(place, seq_of * feats, norm_gains, tokens, weights)

    n = lax.axis_size("head")
    before = lax.ppermute(kv, "head", [(i, i + 1) for i in range(n - 1)])
    after = lax.ppermute(kv, "head", [(i + 1, i) for i in range(n - 1)])
    scale = HD ** (-0.5) * math.log2(math.e)
    acc = local_call(
        functools.partial(own_kernel, heads, scale),
        jax.ShapeDtypeStruct((heads, rows, 2 * HD), jnp.float32),
        3, 6 * rows * keys * HD * heads, 3 * 2**20, "own_frame",
    )(query, kv, keep[:, keys : 2 * keys])
    sides = jnp.concatenate([keep[:, :keys], keep[:, 2 * keys :]], axis=1)
    head_out = local_call(
        functools.partial(rest_kernel, heads, scale),
        jax.ShapeDtypeStruct((rows, width), BF),
        5, 12 * rows * keys * HD * heads, 4 * 2**20, "other_frames",
    )(query, before, after, sides, acc)
    pieces = (head_out,) + ring_x(head_out)
    return output_projection(seq_of * width, pieces, out_all)


def solution(mesh):
    placed = (
        P(("dp", "head"), "seq"),
        P("head", None, "seq"),
        P(),
        P("seq", "head"),
        P(("dp", "head"), None),
    )
    return jax.shard_map(
        per_device, mesh=mesh, in_specs=placed, out_specs=P(("dp", "head"), "seq"), check_vma=False
    )
```

time: 286 us -> 148 us (0.52)
  the two profiles are of different devices: /device:TPU:1 before, /device:TPU:94 now
where the time goes in v1:
time: 148 us; the launch traced here: 147 us
  waiting for transfers between devices  63.1 us (43%)
  starting transfers between devices  42.9 us (29%)
  Pallas kernels  16.9 us (11%)
  between operations  13.6 us (9%)
  local copies, waits for them, and re-layouts  10.6 us (7%)
    ppermute x8, waiting for transfers between devices, along(): return lax.ppermute(x, axis, [(i, (i + step) % n) for i in range(n)])  25.9 us
    ppermute x10, starting transfers between devices, moved(): return lax.ppermute(x, ('dp', 'head'), pairs)  16.3 us
    ppermute x10, waiting for transfers between devices, moved(): return lax.ppermute(x, ('dp', 'head'), pairs)  15 us
    ppermute x1, waiting for transfers between devices, per_device(): before = lax.ppermute(kv, 'head', [(i, i + 1) for i in range(n - 1)])  12.8 us
    pallas_call x1, Pallas kernels, project(): pl.pallas_call(functools.partial(project_kernel, rows), out_shape=(jax.Sh...  10.8 us
    ppermute x8, starting transfers between devices, swapped(): return lax.ppermute(x, 'dp', [(0, 1), (1, 0)])  10.1 us
    unnamed x39, local copies, waits for them, and re-layouts  8.6 us
    ppermute x8, starting transfers between devices, along(): return lax.ppermute(x, axis, [(i, (i + step) % n) for i in range(n)])  7.61 us
  transfers between devices with their start and end apart: 29, of which 16 were waited for; matrix products, arithmetic and copies ran while one was open for 2% of the time, Pallas kernels for 9%

profile of v1, /device:TPU:94, one launch (start us, length us, event | category | flops | bytes accessed | tf_op | source)
XLA Modules:
  0.0 147.2 jit_solution(1567502011625367785)
XLA Ops:
  8.8 3.2 %collective-permute-start.4 = (bf16[3,48,384]{2,1,0:T(8,128)(2,1)S(1)}, bf16[3,48,384]{2,1,0:T(8,128)(2,1)S(1)}, u32[]{:S(2)}, u32[]{:S(2)}) collective-permute-start(bf16[3,48,384]{2,1,0:T(8,128)(2,1)S(1)} %dynamic-slice_bitcast_fusion), channel_id=1, source_target_pairs={{0,1},{1,2},{2,3},{3,0},{4,5},{5,6},{6,7},{7,4},{8,9},{9,10},{10,1... | collective-permute-start | bytes 331784 | tf_op jit(solution)/shard_map/ppermute | solution.py:34
  15.1 2.0 %collective-permute-start.7 = (bf16[3,192,384]{2,1,0:T(8,128)(2,1)S(1)}, bf16[3,192,384]{2,1,0:T(8,128)(2,1)S(1)}, u32[]{:S(2)}, u32[]{:S(2)}) collective-permute-start(bf16[3,192,384]{2,1,0:T(8,128)(2,1)S(1)} %pad_maximum_fusion.refs_6_), channel_id=1, source_target_pairs={{0,4},{1,5},{2,6},{3,7},{4,8},{5,9},{6,10},{7,11},{8,12},{9,13},{1... | collective-permute-start | bytes 1327112 | tf_op jit(solution)/shard_map/ppermute | solution.py:34
  17.6 6.2 %collective-permute-done.7.refs_7_ = bf16[3,192,384]{2,1,0:T(8,128)(2,1)S(1)} collective-permute-done((bf16[3,192,384]{2,1,0:T(8,128)(2,1)S(1)}, bf16[3,192,384]{2,1,0:T(8,128)(2,1)S(1)}, u32[]{:S(2)}, u32[]{:S(2)}) %collective-permute-start.7) | collective-permute-done | bytes 442400 | tf_op jit(solution)/shard_map/ppermute | solution.py:34
  23.9 2.2 %collective-permute-start.9 = (bf16[3,192,384]{2,1,0:T(8,128)(2,1)S(1)}, bf16[3,192,384]{2,1,0:T(8,128)(2,1)S(1)}, u32[]{:S(2)}, u32[]{:S(2)}) collective-permute-start(bf16[3,192,384]{2,1,0:T(8,128)(2,1)S(1)} %collective-permute-done.7.refs_7_), channel_id=1, source_target_pairs={{0,4},{1,5},{2,6},{3,7},{4,8},{5,9},{6,10},{7,11},{8,12},{9,13},{1... | collective-permute-start | bytes 1327112 | tf_op jit(solution)/shard_map/ppermute | solution.py:34
  26.8 5.2 %collective-permute-done.8.refs_8_ = bf16[3,192,384]{2,1,0:T(8,128)(2,1)S(1)} collective-permute-done((bf16[3,192,384]{2,1,0:T(8,128)(2,1)S(1)}, bf16[3,192,384]{2,1,0:T(8,128)(2,1)S(1)}, u32[]{:S(2)}, u32[]{:S(2)}) %collective-permute-start.8) | collective-permute-done | bytes 442400 | tf_op jit(solution)/shard_map/ppermute | solution.py:34
  32.7 3.7 %collective-permute-start.11 = (bf16[3,192,384]{2,1,0:T(8,128)(2,1)S(1)}, bf16[3,192,384]{2,1,0:T(8,128)(2,1)S(1)}, u32[]{:S(2)}, u32[]{:S(2)}) collective-permute-start(bf16[3,192,384]{2,1,0:T(8,128)(2,1)S(1)} %collective-permute-done.9.refs_9_), channel_id=1, source_target_pairs={{0,4},{1,5},{2,6},{3,7},{4,8},{5,9},{6,10},{7,11},{8,12},{9,13},{1... | collective-permute-start | bytes 1327112 | tf_op jit(solution)/shard_map/ppermute | solution.py:34
  36.4 4.6 %collective-permute-start.14 = (bf16[3,192,384]{2,1,0:T(8,128)(2,1)S(1)}, bf16[3,192,384]{2,1,0:T(8,128)(2,1)S(1)}, u32[]{:S(2)}, u32[]{:S(2)}) collective-permute-start(bf16[3,192,384]{2,1,0:T(8,128)(2,1)S(1)} %pad_maximum_fusion.refs_6_), channel_id=1, source_target_pairs={{0,128},{128,0},{1,129},{129,1},{2,130},{130,2},{3,131},{131,3},{4... | collective-permute-start | bytes 1327112 | tf_op jit(solution)/shard_map/ppermute | solution.py:43
  41.0 1.9 %collective-permute-done.1.refs_3_ = bf16[512,768]{1,0:T(8,128)(2,1)S(1)} collective-permute-done((bf16[512,768]{1,0:T(8,128)(2,1)}, bf16[512,768]{1,0:T(8,128)(2,1)S(1)}, u32[]{:S(2)}, u32[]{:S(2)}) %collective-permute-start.1) | collective-permute-done | bytes 786464 | tf_op jit(solution)/shard_map/ppermute | solution.py:39
  42.9 4.8 %collective-permute-start.16 = (bf16[3,192,384]{2,1,0:T(8,128)(2,1)S(1)}, bf16[3,192,384]{2,1,0:T(8,128)(2,1)}, u32[]{:S(2)}, u32[]{:S(2)}) collective-permute-start(bf16[3,192,384]{2,1,0:T(8,128)(2,1)S(1)} %collective-permute-done.8.refs_8_), channel_id=1, source_target_pairs={{0,128},{128,0},{1,129},{129,1},{2,130},{130,2},{3,131},{131,3},{4... | collective-permute-start | bytes 1327112 | tf_op jit(solution)/shard_map/ppermute | solution.py:43
  47.7 3.8 %collective-permute-start.13 = (bf16[3,192,384]{2,1,0:T(8,128)(2,1)S(1)}, bf16[3,192,384]{2,1,0:T(8,128)(2,1)}, u32[]{:S(2)}, u32[]{:S(2)}) collective-permute-start(bf16[3,192,384]{2,1,0:T(8,128)(2,1)S(1)} %collective-permute-done.11.refs_11_), channel_id=1, source_target_pairs={{0,4},{1,5},{2,6},{3,7},{4,8},{5,9},{6,10},{7,11},{8,12},{9,13},{1... | collective-permute-start | bytes 1327112 | tf_op jit(solution)/shard_map/ppermute | solution.py:34
  54.6 2.0 %collective-permute-start.3 = (bf16[256,768]{1,0:T(8,128)(2,1)}, bf16[256,768]{1,0:T(8,128)(2,1)}, u32[]{:S(2)}, u32[]{:S(2)}) collective-permute-start(bf16[256,768]{1,0:T(8,128)(2,1)} %slice.29), channel_id=1, source_target_pairs={{0,96},{32,0},{64,32},{96,64},{1,97},{33,1},{65,33},{97,65},{2,98}... | collective-permute-start | bytes 1179656 | tf_op jit(solution)/shard_map/ppermute | solution.py:39
  57.0 7.6 %collective-permute-done.2.refs_4_ = bf16[256,768]{1,0:T(8,128)(2,1)S(1)} collective-permute-done((bf16[256,768]{1,0:T(8,128)(2,1)}, bf16[256,768]{1,0:T(8,128)(2,1)S(1)}, u32[]{:S(2)}, u32[]{:S(2)}) %collective-permute-start.2) | collective-permute-done | bytes 393248 | tf_op jit(solution)/shard_map/ppermute | solution.py:39
  64.6 2.1 %collective-permute-done.3.refs_5_ = bf16[256,768]{1,0:T(8,128)(2,1)} collective-permute-done((bf16[256,768]{1,0:T(8,128)(2,1)}, bf16[256,768]{1,0:T(8,128)(2,1)}, u32[]{:S(2)}, u32[]{:S(2)}) %collective-permute-start.3) | collective-permute-done | bytes 393248 | tf_op jit(solution)/shard_map/ppermute | solution.py:39
  73.8 10.8 %project.1 = (bf16[512,384]{1,0:T(8,128)(2,1)S(1)}, bf16[512,768]{1,0:T(8,128)(2,1)}) custom-call(s32[64]{0:T(128)S(1)} %stack.280.place, s32[5]{0:T(128)S(1)} %get-tuple-element.12.token_place, f32[2,128]{1,0:T(2,128)S(1)} %copy-done.9, bf16[512,768]{1,0:T(8,128)(2,1)} %refs_1_.1, bf16[512,768]{1,0:T(8,128)(2,1)} %copy-done.10, ...), custom_call_target="tpu_custom_call" | custom-call | flops 3623878656 | bytes 12582912 | tf_op jit(solution)/shard_map/project/pallas_call | solution.py:134
  84.7 6.9 %collective-permute-start.22 = (bf16[512,768]{1,0:T(8,128)(2,1)}, bf16[512,768]{1,0:T(8,128)(2,1)S(1)}, u32[]{:S(2)}, u32[]{:S(2)}) collective-permute-start(bf16[512,768]{1,0:T(8,128)(2,1)} %get-tuple-element.8.kv_ref), channel_id=1, source_target_pairs={{0,1},{1,2},{2,3},{3,4},{4,5},{5,6},{6,7},{7,8},{8,9},{9,10},{10,1... | collective-permute-start | bytes 2359304 | tf_op jit(solution)/shard_map/ppermute | solution.py:267
  91.6 1.9 %collective-permute-start.23 = (bf16[512,768]{1,0:T(8,128)(2,1)}, bf16[512,768]{1,0:T(8,128)(2,1)S(1)}, u32[]{:S(2)}, u32[]{:S(2)}) collective-permute-start(bf16[512,768]{1,0:T(8,128)(2,1)} %get-tuple-element.8.kv_ref), channel_id=1, source_target_pairs={{1,0},{2,1},{3,2},{4,3},{5,4},{6,5},{7,6},{8,7},{9,8},{10,9},{11,1... | collective-permute-start | bytes 2359304 | tf_op jit(solution)/shard_map/ppermute | solution.py:268
  96.2 12.8 %collective-permute-done.22.before_ref = bf16[512,768]{1,0:T(8,128)(2,1)S(1)} collective-permute-done((bf16[512,768]{1,0:T(8,128)(2,1)}, bf16[512,768]{1,0:T(8,128)(2,1)S(1)}, u32[]{:S(2)}, u32[]{:S(2)}) %collective-permute-start.22) | collective-permute-done | bytes 786464 | tf_op jit(solution)/shard_map/ppermute | solution.py:267
  109.0 6.1 %collective-permute-done.23.after_ref = bf16[512,768]{1,0:T(8,128)(2,1)S(1)} collective-permute-done((bf16[512,768]{1,0:T(8,128)(2,1)}, bf16[512,768]{1,0:T(8,128)(2,1)S(1)}, u32[]{:S(2)}, u32[]{:S(2)}) %collective-permute-start.23) | collective-permute-done | bytes 786464 | tf_op jit(solution)/shard_map/ppermute | solution.py:268
  115.1 1.9 %other_frames.1.own = bf16[512,384]{1,0:T(8,128)(2,1)S(1)} custom-call(bf16[512,384]{1,0:T(8,128)(2,1)S(1)} %get-tuple-element.7.q_ref, bf16[512,768]{1,0:T(8,128)(2,1)S(1)} %collective-permute-done.22.before_ref, bf16[512,768]{1,0:T(8,128)(2,1)S(1)} %collective-permute-done.23.after_ref, f32[4,1024]{1,0:T(4,128)S(1)} %pad_maximum_fusion.1.keep_ref, ...), custom_call_target="tpu_custom_call" | custom-call | flops 1207959552 | bytes 4194304 | tf_op jit(solution)/shard_map/other_frames/pallas_call | solution.py:276
  117.2 2.0 %collective-permute-start.25 = (bf16[512,384]{1,0:T(8,128)(2,1)S(1)}, bf16[512,384]{1,0:T(8,128)(2,1)S(1)}, u32[]{:S(2)}, u32[]{:S(2)}) collective-permute-start(bf16[512,384]{1,0:T(8,128)(2,1)S(1)} %other_frames.1.own), channel_id=1, source_target_pairs={{0,96},{32,0},{64,32},{96,64},{1,97},{33,1},{65,33},{97,65},{2,98}... | collective-permute-start | bytes 1179656 | tf_op jit(solution)/shard_map/ppermute | solution.py:39
  119.1 8.0 %collective-permute-done.24.below = bf16[512,384]{1,0:T(8,128)(2,1)S(1)} collective-permute-done((bf16[512,384]{1,0:T(8,128)(2,1)S(1)}, bf16[512,384]{1,0:T(8,128)(2,1)S(1)}, u32[]{:S(2)}, u32[]{:S(2)}) %collective-permute-start.24) | collective-permute-done | bytes 393248 | tf_op jit(solution)/shard_map/ppermute | solution.py:39
  129.3 3.5 %collective-permute-done.26.far_top = bf16[256,384]{1,0:T(8,128)(2,1)S(1)} collective-permute-done((bf16[256,384]{1,0:T(8,128)(2,1)S(1)}, bf16[256,384]{1,0:T(8,128)(2,1)S(1)}, u32[]{:S(2)}, u32[]{:S(2)}) %collective-permute-start.26) | collective-permute-done | bytes 196640 | tf_op jit(solution)/shard_map/ppermute | solution.py:39
  132.9 2.8 %collective-permute-done.27.far_bottom = bf16[256,384]{1,0:T(8,128)(2,1)S(1)} collective-permute-done((bf16[256,384]{1,0:T(8,128)(2,1)S(1)}, bf16[256,384]{1,0:T(8,128)(2,1)S(1)}, u32[]{:S(2)}, u32[]{:S(2)}) %collective-permute-start.27) | collective-permute-done | bytes 196640 | tf_op jit(solution)/shard_map/ppermute | solution.py:39
  137.3 3.0 %output.1 = bf16[512,768]{1,0:T(8,128)(2,1)} custom-call(s32[5]{0:T(128)S(1)} %get-tuple-element.13.place, bf16[512,384]{1,0:T(8,128)(2,1)S(1)} %other_frames.1.own, bf16[512,384]{1,0:T(8,128)(2,1)S(1)} %collective-permute-done.24.below, bf16[512,384]{1,0:T(8,128)(2,1)S(1)} %collective-permute-done.25.above, ...), custom_call_target="tpu_custom_call" | custom-call | flops 1207959552 | bytes 5242880 | tf_op jit(solution)/shard_map/output/pallas_call | solution.py:226
  (94 shorter events, 24.7 us)
Async XLA Ops:
  6.5 129.1 %all-gather.2.cloned.1.call-start = ((), (), s32[]{:S(2)}) async-start(), calls=%async_computation | async-start | bytes 2433024 | tf_op jit(solution)/shard_map/all_gather | solution.py:259
  7.5 6.4 %collective-permute-start.6 = (bf16[3,48,384]{2,1,0:T(8,128)(2,1)S(1)}, bf16[3,48,384]{2,1,0:T(8,128)(2,1)S(1)}, u32[]{:S(2)}, u32[]{:S(2)}) collective-permute-start(bf16[3,48,384]{2,1,0:T(8,128)(2,1)S(1)} %dynamic-slice_bitcast_fusion), channel_id=1, source_target_pairs={{0,2},{1,3},{2,0},{3,1},{4,6},{5,7},{6,4},{7,5},{8,10},{9,11},{10,... | collective-permute-start | bytes 331784 | tf_op jit(solution)/shard_map/ppermute | solution.py:34
  8.8 6.2 %collective-permute-start.5 = (bf16[3,48,384]{2,1,0:T(8,128)(2,1)S(1)}, bf16[3,48,384]{2,1,0:T(8,128)(2,1)S(1)}, u32[]{:S(2)}, u32[]{:S(2)}) collective-permute-start(bf16[3,48,384]{2,1,0:T(8,128)(2,1)S(1)} %dynamic-slice_bitcast_fusion), channel_id=1, source_target_pairs={{0,3},{1,0},{2,1},{3,2},{4,7},{5,4},{6,5},{7,6},{8,11},{9,8},{10,9... | collective-permute-start | bytes 331784 | tf_op jit(solution)/shard_map/ppermute | solution.py:34
  8.8 6.2 %collective-permute-start.4 = (bf16[3,48,384]{2,1,0:T(8,128)(2,1)S(1)}, bf16[3,48,384]{2,1,0:T(8,128)(2,1)S(1)}, u32[]{:S(2)}, u32[]{:S(2)}) collective-permute-start(bf16[3,48,384]{2,1,0:T(8,128)(2,1)S(1)} %dynamic-slice_bitcast_fusion), channel_id=1, source_target_pairs={{0,1},{1,2},{2,3},{3,0},{4,5},{5,6},{6,7},{7,4},{8,9},{9,10},{10,1... | collective-permute-start | bytes 331784 | tf_op jit(solution)/shard_map/ppermute | solution.py:34
  15.1 8.8 %collective-permute-start.7 = (bf16[3,192,384]{2,1,0:T(8,128)(2,1)S(1)}, bf16[3,192,384]{2,1,0:T(8,128)(2,1)S(1)}, u32[]{:S(2)}, u32[]{:S(2)}) collective-permute-start(bf16[3,192,384]{2,1,0:T(8,128)(2,1)S(1)} %pad_maximum_fusion.refs_6_), channel_id=1, source_target_pairs={{0,4},{1,5},{2,6},{3,7},{4,8},{5,9},{6,10},{7,11},{8,12},{9,13},{1... | collective-permute-start | bytes 1327112 | tf_op jit(solution)/shard_map/ppermute | solution.py:34
  17.1 23.9 %collective-permute-start = (bf16[512,768]{1,0:T(8,128)(2,1)}, bf16[512,768]{1,0:T(8,128)(2,1)S(1)}, u32[]{:S(2)}, u32[]{:S(2)}) collective-permute-start(bf16[512,768]{1,0:T(8,128)(2,1)} %refs_1_.1), channel_id=1, source_target_pairs={{0,32},{32,64},{64,96},{96,0},{1,33},{33,65},{65,97},{97,1},{2,34}... | collective-permute-start | bytes 2359304 | tf_op jit(solution)/shard_map/ppermute | solution.py:39
  17.5 14.5 %collective-permute-start.8 = (bf16[3,192,384]{2,1,0:T(8,128)(2,1)S(1)}, bf16[3,192,384]{2,1,0:T(8,128)(2,1)S(1)}, u32[]{:S(2)}, u32[]{:S(2)}) collective-permute-start(bf16[3,192,384]{2,1,0:T(8,128)(2,1)S(1)} %pad_maximum_fusion.refs_6_), channel_id=1, source_target_pairs={{0,28},{1,29},{2,30},{3,31},{4,0},{5,1},{6,2},{7,3},{8,4},{9,5},{1... | collective-permute-start | bytes 1327112 | tf_op jit(solution)/shard_map/ppermute | solution.py:34
  23.9 8.8 %collective-permute-start.9 = (bf16[3,192,384]{2,1,0:T(8,128)(2,1)S(1)}, bf16[3,192,384]{2,1,0:T(8,128)(2,1)S(1)}, u32[]{:S(2)}, u32[]{:S(2)}) collective-permute-start(bf16[3,192,384]{2,1,0:T(8,128)(2,1)S(1)} %collective-permute-done.7.refs_7_), channel_id=1, source_target_pairs={{0,4},{1,5},{2,6},{3,7},{4,8},{5,9},{6,10},{7,11},{8,12},{9,13},{1... | collective-permute-start | bytes 1327112 | tf_op jit(solution)/shard_map/ppermute | solution.py:34
  26.0 16.9 %collective-permute-start.1 = (bf16[512,768]{1,0:T(8,128)(2,1)}, bf16[512,768]{1,0:T(8,128)(2,1)S(1)}, u32[]{:S(2)}, u32[]{:S(2)}) collective-permute-start(bf16[512,768]{1,0:T(8,128)(2,1)} %refs_1_.1), channel_id=1, source_target_pairs={{0,96},{32,0},{64,32},{96,64},{1,97},{33,1},{65,33},{97,65},{2,98}... | collective-permute-start | bytes 2359304 | tf_op jit(solution)/shard_map/ppermute | solution.py:39
  32.0 15.7 %collective-permute-start.10 = (bf16[3,192,384]{2,1,0:T(8,128)(2,1)S(1)}, bf16[3,192,384]{2,1,0:T(8,128)(2,1)S(1)}, u32[]{:S(2)}, u32[]{:S(2)}) collective-permute-start(bf16[3,192,384]{2,1,0:T(8,128)(2,1)S(1)} %collective-permute-done.8.refs_8_), channel_id=1, source_target_pairs={{0,28},{1,29},{2,30},{3,31},{4,0},{5,1},{6,2},{7,3},{8,4},{9,5},{1... | collective-permute-start | bytes 1327112 | tf_op jit(solution)/shard_map/ppermute | solution.py:34
  32.7 15.0 %collective-permute-start.11 = (bf16[3,192,384]{2,1,0:T(8,128)(2,1)S(1)}, bf16[3,192,384]{2,1,0:T(8,128)(2,1)S(1)}, u32[]{:S(2)}, u32[]{:S(2)}) collective-permute-start(bf16[3,192,384]{2,1,0:T(8,128)(2,1)S(1)} %collective-permute-done.9.refs_9_), channel_id=1, source_target_pairs={{0,4},{1,5},{2,6},{3,7},{4,8},{5,9},{6,10},{7,11},{8,12},{9,13},{1... | collective-permute-start | bytes 1327112 | tf_op jit(solution)/shard_map/ppermute | solution.py:34
  36.4 16.7 %collective-permute-start.14 = (bf16[3,192,384]{2,1,0:T(8,128)(2,1)S(1)}, bf16[3,192,384]{2,1,0:T(8,128)(2,1)S(1)}, u32[]{:S(2)}, u32[]{:S(2)}) collective-permute-start(bf16[3,192,384]{2,1,0:T(8,128)(2,1)S(1)} %pad_maximum_fusion.refs_6_), channel_id=1, source_target_pairs={{0,128},{128,0},{1,129},{129,1},{2,130},{130,2},{3,131},{131,3},{4... | collective-permute-start | bytes 1327112 | tf_op jit(solution)/shard_map/ppermute | solution.py:43
  40.9 12.9 %collective-permute-start.15 = (bf16[3,192,384]{2,1,0:T(8,128)(2,1)S(1)}, bf16[3,192,384]{2,1,0:T(8,128)(2,1)S(1)}, u32[]{:S(2)}, u32[]{:S(2)}) collective-permute-start(bf16[3,192,384]{2,1,0:T(8,128)(2,1)S(1)} %collective-permute-done.7.refs_7_), channel_id=1, source_target_pairs={{0,128},{128,0},{1,129},{129,1},{2,130},{130,2},{3,131},{131,3},{4... | collective-permute-start | bytes 1327112 | tf_op jit(solution)/shard_map/ppermute | solution.py:43
  42.9 14.0 %collective-permute-start.16 = (bf16[3,192,384]{2,1,0:T(8,128)(2,1)S(1)}, bf16[3,192,384]{2,1,0:T(8,128)(2,1)}, u32[]{:S(2)}, u32[]{:S(2)}) collective-permute-start(bf16[3,192,384]{2,1,0:T(8,128)(2,1)S(1)} %collective-permute-done.8.refs_8_), channel_id=1, source_target_pairs={{0,128},{128,0},{1,129},{129,1},{2,130},{130,2},{3,131},{131,3},{4... | collective-permute-start | bytes 1327112 | tf_op jit(solution)/shard_map/ppermute | solution.py:43
  47.7 19.0 %collective-permute-start.12 = (bf16[3,192,384]{2,1,0:T(8,128)(2,1)S(1)}, bf16[3,192,384]{2,1,0:T(8,128)(2,1)}, u32[]{:S(2)}, u32[]{:S(2)}) collective-permute-start(bf16[3,192,384]{2,1,0:T(8,128)(2,1)S(1)} %collective-permute-done.10.refs_10_), channel_id=1, source_target_pairs={{0,28},{1,29},{2,30},{3,31},{4,0},{5,1},{6,2},{7,3},{8,4},{9,5},{1... | collective-permute-start | bytes 1327112 | tf_op jit(solution)/shard_map/ppermute | solution.py:34
  47.7 19.5 %collective-permute-start.13 = (bf16[3,192,384]{2,1,0:T(8,128)(2,1)S(1)}, bf16[3,192,384]{2,1,0:T(8,128)(2,1)}, u32[]{:S(2)}, u32[]{:S(2)}) collective-permute-start(bf16[3,192,384]{2,1,0:T(8,128)(2,1)S(1)} %collective-permute-done.11.refs_11_), channel_id=1, source_target_pairs={{0,4},{1,5},{2,6},{3,7},{4,8},{5,9},{6,10},{7,11},{8,12},{9,13},{1... | collective-permute-start | bytes 1327112 | tf_op jit(solution)/shard_map/ppermute | solution.py:34
  53.8 10.7 %collective-permute-start.2 = (bf16[256,768]{1,0:T(8,128)(2,1)}, bf16[256,768]{1,0:T(8,128)(2,1)S(1)}, u32[]{:S(2)}, u32[]{:S(2)}) collective-permute-start(bf16[256,768]{1,0:T(8,128)(2,1)} %slice.28), channel_id=1, source_target_pairs={{0,32},{32,64},{64,96},{96,0},{1,33},{33,65},{65,97},{97,1},{2,34}... | collective-permute-start | bytes 1179656 | tf_op jit(solution)/shard_map/ppermute | solution.py:39
  54.6 12.1 %collective-permute-start.3 = (bf16[256,768]{1,0:T(8,128)(2,1)}, bf16[256,768]{1,0:T(8,128)(2,1)}, u32[]{:S(2)}, u32[]{:S(2)}) collective-permute-start(bf16[256,768]{1,0:T(8,128)(2,1)} %slice.29), channel_id=1, source_target_pairs={{0,96},{32,0},{64,32},{96,64},{1,97},{33,1},{65,33},{97,65},{2,98}... | collective-permute-start | bytes 1179656 | tf_op jit(solution)/shard_map/ppermute | solution.py:39
  56.9 10.4 %collective-permute-start.17 = (bf16[3,192,384]{2,1,0:T(8,128)(2,1)S(1)}, bf16[3,192,384]{2,1,0:T(8,128)(2,1)S(1)}, u32[]{:S(2)}, u32[]{:S(2)}) collective-permute-start(bf16[3,192,384]{2,1,0:T(8,128)(2,1)S(1)} %collective-permute-done.9.refs_9_), channel_id=1, source_target_pairs={{0,128},{128,0},{1,129},{129,1},{2,130},{130,2},{3,131},{131,3},{4... | collective-permute-start | bytes 1327112 | tf_op jit(solution)/shard_map/ppermute | solution.py:43
  84.7 24.3 %collective-permute-start.22 = (bf16[512,768]{1,0:T(8,128)(2,1)}, bf16[512,768]{1,0:T(8,128)(2,1)S(1)}, u32[]{:S(2)}, u32[]{:S(2)}) collective-permute-start(bf16[512,768]{1,0:T(8,128)(2,1)} %get-tuple-element.8.kv_ref), channel_id=1, source_target_pairs={{0,1},{1,2},{2,3},{3,4},{4,5},{5,6},{6,7},{7,8},{8,9},{9,10},{10,1... | collective-permute-start | bytes 2359304 | tf_op jit(solution)/shard_map/ppermute | solution.py:267
  91.6 23.5 %collective-permute-start.23 = (bf16[512,768]{1,0:T(8,128)(2,1)}, bf16[512,768]{1,0:T(8,128)(2,1)S(1)}, u32[]{:S(2)}, u32[]{:S(2)}) collective-permute-start(bf16[512,768]{1,0:T(8,128)(2,1)} %get-tuple-element.8.kv_ref), channel_id=1, source_target_pairs={{1,0},{2,1},{3,2},{4,3},{5,4},{6,5},{7,6},{8,7},{9,8},{10,9},{11,1... | collective-permute-start | bytes 2359304 | tf_op jit(solution)/shard_map/ppermute | solution.py:268
  117.0 10.1 %collective-permute-start.24 = (bf16[512,384]{1,0:T(8,128)(2,1)S(1)}, bf16[512,384]{1,0:T(8,128)(2,1)S(1)}, u32[]{:S(2)}, u32[]{:S(2)}) collective-permute-start(bf16[512,384]{1,0:T(8,128)(2,1)S(1)} %other_frames.1.own), channel_id=1, source_target_pairs={{0,32},{32,64},{64,96},{96,0},{1,33},{33,65},{65,97},{97,1},{2,34}... | collective-permute-start | bytes 1179656 | tf_op jit(solution)/shard_map/ppermute | solution.py:39
  117.2 11.5 %collective-permute-start.25 = (bf16[512,384]{1,0:T(8,128)(2,1)S(1)}, bf16[512,384]{1,0:T(8,128)(2,1)S(1)}, u32[]{:S(2)}, u32[]{:S(2)}) collective-permute-start(bf16[512,384]{1,0:T(8,128)(2,1)S(1)} %other_frames.1.own), channel_id=1, source_target_pairs={{0,96},{32,0},{64,32},{96,64},{1,97},{33,1},{65,33},{97,65},{2,98}... | collective-permute-start | bytes 1179656 | tf_op jit(solution)/shard_map/ppermute | solution.py:39
  128.7 7.0 %collective-permute-start.27 = (bf16[256,384]{1,0:T(8,128)(2,1)S(1)}, bf16[256,384]{1,0:T(8,128)(2,1)S(1)}, u32[]{:S(2)}, u32[]{:S(2)}) collective-permute-start(bf16[256,384]{1,0:T(8,128)(2,1)S(1)} %slice.34), channel_id=1, source_target_pairs={{0,96},{32,0},{64,32},{96,64},{1,97},{33,1},{65,33},{97,65},{2,98}... | collective-permute-start | bytes 589832 | tf_op jit(solution)/shard_map/ppermute | solution.py:39
  (23 other events, 203.4 us)
Sparse Core Ops, SparseCore 0:
  9.9 78.1 all-gather.1
